TPU v7x, 32 devices: a whole 2x2x4 slice. The times are simulated.
32 devices in a mesh: rows: 4 (over y, x), cols: 4 (over z), depth: 2 (over core).
Axes of the slice: x: 2, y: 2, z: 4, core: 2. Of those that a mesh axis runs over, the one named last changes fastest.
Arguments:
- tile_left: float32 [4, 4, 64, 2048], P('rows', 'cols'), may hold values from -6 to 6
- tile_right: float32 [4, 4, 64, 2048], P('rows', 'cols'), may hold values from -0.75 to 0.75
- left_u: bfloat16 [2, 16, 4, 64, 2048], P('depth', 'cols', 'rows'), may hold values from -6 to 6
- left_v: bfloat16 [2, 16, 4, 64, 2048], P('depth', 'cols', 'rows'), may hold values from -0.0625 to 0.0625
- rank_left: int32 [2, 16, 4], P('depth', 'cols', 'rows'), may hold values from 16 to 64
- right_u: bfloat16 [2, 16, 4, 64, 2048], P('depth', 'rows', 'cols'), may hold values from -6 to 6
- right_v: bfloat16 [2, 16, 4, 64, 2048], P('depth', 'rows', 'cols'), may hold values from -0.0625 to 0.0625
- rank_right: int32 [2, 16, 4], P('depth', 'rows', 'cols'), may hold values from 16 to 64
- triples: int32 [4, 4, 2, 6], P('rows', 'cols', 'depth'), may hold values from -1 to 15, as said below
Outputs:
- new_left: float32 [4, 4, 64, 2048], P('rows', 'cols', None, 'depth')
- new_right: float32 [4, 4, 64, 2048], P('rows', 'cols', None, 'depth')
Inputs may be any that keep to these rules, and one draw needn't show every extreme that they name: `triples`: for each tile and layer the first entries are distinct panel numbers of 0 to 15 and the remaining entries are -1; every list has at least one panel number, and in every draw some tile in some layer lists all 6.
All inputs are finite; a program needn't handle non-finite values.
Results may differ from a plain program's by a relative error of at most 0.0043.
Values may be sent and summed in bfloat16 or wider, within the bound.
A program may use at most 128 MiB of HBM per device.

v0:
```python
import math

import jax
import jax.numpy as jnp
import ml_dtypes
import numpy as np
from jax import lax
from jax.experimental import pallas as pl
from jax.experimental.pallas import tpu as pltpu
from jax.sharding import PartitionSpec as P

HIGHEST = lax.Precision.HIGHEST
LANES = 128
SUB = 8


def dot(first, second, dims=(1, 0), precision=HIGHEST):
    return lax.dot_general(
        first,
        second,
        (((dims[0],), (dims[1],)), ((), ())),
        precision=precision,
        preferred_element_type=jnp.float32,
    )


def start_table(rank, width):
    freq = np.arange(1, rank + 1, dtype=np.int64)[:, None]
    cell = 2 * np.arange(width, dtype=np.int64)[None, :] + 1
    table = np.cos((freq * cell % (4 * width)) * (math.pi / (2 * width))).astype(np.float32)
    high = table.astype(ml_dtypes.bfloat16)
    low = (table - high.astype(np.float32)).astype(ml_dtypes.bfloat16)
    return np.concatenate([high, low], axis=0)


def split(value):
    high = value.astype(jnp.bfloat16)
    return high, (value - high.astype(jnp.float32)).astype(jnp.bfloat16)


def inverse_factor(image, coeff):
    rank = coeff.shape[0]
    wide = dot(image, jnp.concatenate([coeff, coeff], axis=0), (1, 1))
    row = lax.broadcasted_iota(jnp.int32, wide.shape, 0)
    lane = lax.broadcasted_iota(jnp.int32, wide.shape, 1)
    diag = lane == row + rank
    trace = jnp.sum(jnp.where(diag, wide, 0.0))
    shift = 1e-05 * trace / rank + 1e-06
    work = jnp.where(
        lane >= rank,
        wide + jnp.where(diag, shift, 0.0),
        jnp.where(lane == row, 1.0, 0.0),
    )
    count = rank // SUB
    blocks = [work[SUB * b : SUB * (b + 1)] for b in range(count)]
    below = lax.broadcasted_iota(jnp.int32, (SUB, 2 * rank), 0)
    for p in range(count):
        cols = [
            {
                b: jnp.broadcast_to(
                    blocks[b][:, rank + SUB * p + t : rank + SUB * p + t + 1], (SUB, 2 * rank)
                )
                for b in range(p, count)
            }
            for t in range(SUB)
        ]
        for t in range(SUB):
            inverse = 1.0 / cols[t][p][t : t + 1]
            factor = {b: cols[t][b] * inverse for b in range(p, count)}
            factor[p] = jnp.where(below > t, factor[p], 0.0)
            for u in range(t + 1, SUB):
                top = cols[u][p][t : t + 1]
                for b in range(p, count):
                    cols[u][b] = cols[u][b] - factor[b] * top
            lead = blocks[p][t : t + 1]
            for b in range(p, count):
                blocks[b] = blocks[b] - factor[b] * lead
    work = jnp.concatenate(blocks, axis=0)
    pivots = jnp.sum(jnp.where(diag, work, 0.0), axis=1, keepdims=True)
    return (work / jnp.sqrt(pivots))[:, :rank]


def sweeps(seen, gram_left, gram_right, to_right, to_left):
    for _ in range(2):
        coeff = to_right(seen)
        image = dot(coeff, gram_right)
        seen = dot(inverse_factor(image, coeff), image)
        coeff = to_left(seen)
        image = dot(coeff, gram_left)
        inverse = inverse_factor(image, coeff)
        seen = dot(inverse, image)
    return dot(inverse, coeff), to_right(seen)


def layer_kernel(layers, triples, tl, tr, inner, table, lu, ru, out, xs, ys, kmat, sems):
    rank = tl.shape[0]
    slots = triples.shape[0]
    copies = []
    for slot in range(slots):
        chosen = jnp.maximum(triples[slot], 0)
        place = pl.ds((2 + slot) * rank, rank)
        for side, (src, dst) in enumerate(((lu, xs), (ru, ys))):
            copy = pltpu.make_async_copy(src.at[chosen], dst.at[place], sems.at[side, slot])
            copy.start()
            copies.append(copy)
    for src, dst in ((tl, xs), (tr, ys)):
        high, low = split(src[...])
        dst[pl.ds(0, rank)] = high
        dst[pl.ds(rank, rank)] = low
    shape = (rank, 2 * rank)
    row = lax.broadcasted_iota(jnp.int32, shape, 0)
    lane = lax.broadcasted_iota(jnp.int32, shape, 1)
    pair = jnp.where((lane == row) | (lane == row + rank), 1.0 / layers, 0.0)
    kmat[0, pl.ds(0, rank)] = pair
    kmat[0, pl.ds(rank, rank)] = pair
    for slot in range(slots):
        panel = triples[slot]
        valid = jnp.where(panel >= 0, -1.0, 0.0)
        block = inner[jnp.maximum(panel, 0)].astype(jnp.float32) * valid
        half = slot % 2
        mine = (lane >= rank) if half else (lane < rank)
        kmat[1 + slot // 2, pl.ds(half * rank, rank)] = jnp.where(mine, block, 0.0)
    for copy in copies:
        copy.wait()
    left = xs[...]
    right = ys[...]
    gram_left = dot(left, left, (1, 1), None)
    gram_right = dot(right, right, (1, 1), None)
    seen = dot(table[...], left, (1, 1), None)
    seen = seen[:rank] + seen[rank:]
    pairs = kmat.shape[0]

    def to_right(value):
        return jnp.concatenate(
            [dot(value[:, LANES * b : LANES * (b + 1)], kmat[b]) for b in range(pairs)], axis=1
        )

    def to_left(value):
        return jnp.concatenate(
            [dot(value[:, LANES * b : LANES * (b + 1)], kmat[b], (1, 1)) for b in range(pairs)],
            axis=1,
        )

    probe, image = sweeps(seen, gram_left, gram_right, to_right, to_left)
    for index, (coeff, stack) in enumerate(((probe, xs), (image, ys))):
        both = dot(jnp.concatenate(split(coeff), axis=0), stack[...], (1, 0), None)
        out[index] = both[:rank] + both[rank:]


def join_kernel(share, upper, mine, other, table, new_left, new_right):
    rank = mine.shape[1]
    width = mine.shape[2]
    is_upper = upper[0] == 1
    stacks = []
    for index in range(2):
        a, b = mine[index], other[index]
        stacks.append(
            jnp.concatenate([jnp.where(is_upper, b, a), jnp.where(is_upper, a, b)], axis=0)
        )
    left, right = stacks
    gram_left = dot(left, left, (1, 1))
    gram_right = dot(right, right, (1, 1))
    start = table[pl.ds(0, rank)].astype(jnp.float32) + table[pl.ds(rank, rank)].astype(jnp.float32)
    seen = dot(start, left, (1, 1))
    probe, image = sweeps(seen, gram_left, gram_right, lambda v: v, lambda v: v)
    scale = math.sqrt(width)
    left = jnp.where(is_upper, left[:, share:], left[:, :share])
    right = jnp.where(is_upper, right[:, share:], right[:, :share])
    new_left[0, 0] = dot(probe, left) * scale
    new_right[0, 0] = dot(image, right) / scale


def gathered(left_u, left_v, rank_left, right_u, right_v, rank_right):
    row_u, row_v, row_rank = (
        lax.all_gather(x, "cols", axis=1, tiled=True)[0, :, 0] for x in (left_u, left_v, rank_left)
    )
    col_u, col_v, col_rank = (
        lax.all_gather(x, "rows", axis=1, tiled=True)[0, :, 0]
        for x in (right_u, right_v, rank_right)
    )
    rank = row_v.shape[1]
    index = jnp.arange(rank)
    inner = jnp.einsum("kan,kbn->kab", row_v, col_v, preferred_element_type=jnp.float32)
    keep = (index[None, :, None] < row_rank[:, None, None]) & (
        index[None, None, :] < col_rank[:, None, None]
    )
    inner = jnp.where(keep, inner, 0.0).astype(jnp.bfloat16)
    return row_u, col_u, jnp.concatenate([inner, inner], axis=2)


def shards(tile_left, tile_right, left_u, left_v, rank_left, right_u, right_v, rank_right, triples):
    layers = lax.axis_size("depth")
    rank, width = tile_left.shape[2:]
    slots = triples.shape[3]
    share = width // layers
    row_u, col_u, inner = gathered(left_u, left_v, rank_left, right_u, right_v, rank_right)
    table = jnp.asarray(start_table(rank, width))
    smem = pl.BlockSpec(memory_space=pltpu.SMEM)
    vmem = pl.BlockSpec(memory_space=pltpu.VMEM)
    hbm = pl.BlockSpec(memory_space=pl.ANY)
    stack = (2 + slots) * rank
    params = pltpu.CompilerParams(vmem_limit_bytes=56 * 2**20)
    factors = pl.pallas_call(
        lambda *refs: layer_kernel(layers, *refs),
        out_shape=jax.ShapeDtypeStruct((2, rank, width), jnp.float32),
        in_specs=[smem, vmem, vmem, vmem, vmem, hbm, hbm],
        out_specs=vmem,
        scratch_shapes=[
            pltpu.VMEM((stack, width), jnp.bfloat16),
            pltpu.VMEM((stack, width), jnp.bfloat16),
            pltpu.VMEM((stack // LANES, LANES, LANES), jnp.float32),
            pltpu.SemaphoreType.DMA((2, slots)),
        ],
        compiler_params=params,
        name="layer",
    )(triples[0, 0, 0], tile_left[0, 0], tile_right[0, 0], inner, table, row_u, col_u)
    other = lax.ppermute(factors, "depth", [(d, d ^ 1) for d in range(layers)])
    upper = lax.axis_index("depth").astype(jnp.int32).reshape(1)
    out = jax.ShapeDtypeStruct((1, 1, rank, share), jnp.float32)
    return pl.pallas_call(
        lambda *refs: join_kernel(share, *refs),
        out_shape=(out, out),
        in_specs=[smem, vmem, vmem, vmem],
        out_specs=(vmem, vmem),
        compiler_params=params,
        name="join",
    )(upper, factors, other, table)


def solution(mesh):
    in_specs = (
        P("rows", "cols", None, None),
        P("rows", "cols", None, None),
        P("depth", "cols", "rows", None, None),
        P("depth", "cols", "rows", None, None),
        P("depth", "cols", "rows"),
        P("depth", "rows", "cols", None, None),
        P("depth", "rows", "cols", None, None),
        P("depth", "rows", "cols"),
        P("rows", "cols", "depth", None),
    )
    out_specs = (P("rows", "cols", None, "depth"), P("rows", "cols", None, "depth"))
    return jax.shard_map(shards, mesh=mesh, in_specs=in_specs, out_specs=out_specs, check_vma=False)
```

profile of v0, /device:TPU:0, one launch (start us, length us, event | category | flops | bytes accessed | tf_op | source)
XLA Modules:
  0.0 331.5 jit_solution(1233669470478866921)
XLA Ops:
  7.2 0.0 copy-start.4
  7.2 0.0 copy-start.3
  7.2 0.0 copy-start.1
  7.2 0.0 copy-start.2
  7.2 0.0 all-gather.5.cloned.1.call-start
  7.3 0.7 all-gather.5.cloned.1.call-update
  7.9 0.0 all-gather.7.cloned.1.call-start
  8.0 0.7 all-gather.7.cloned.1.call-update
  8.7 0.0 all-gather.9.cloned.1.call-start
  8.7 0.7 all-gather.9.cloned.1.call-update
  9.4 0.0 all-gather.11.cloned.1.call-start
  9.5 0.5 all-gather.11.cloned.1.call-update
  10.0 0.0 copy-done.4
  10.0 0.6 dynamic-slice.1
  11.3 0.0 copy-done.1
  11.3 0.1 bitcast_dynamic-update-slice_fusion
  11.4 8.8 %all-reduce.1 = s32[16]{0:T(128)S(1)} all-reduce(s32[16]{0:T(128)S(1)} %bitcast_dynamic-update-slice_fusion), channel_id=1, replica_groups=mesh['rows'=4,'cols'=4,'depth'=2] {'rows'}, use_global_device_ids=true, to_apply=%add.1 | all-reduce | flops 16 | bytes 128
  20.2 0.0 copy-done.3
  20.2 0.6 dynamic-slice
  21.4 0.0 copy-done.2
  21.5 0.1 bitcast_dynamic-update-slice_fusion.1
  21.6 8.6 %all-reduce = s32[16]{0:T(128)S(1)} all-reduce(s32[16]{0:T(128)S(1)} %bitcast_dynamic-update-slice_fusion.1), channel_id=1, replica_groups=mesh['rows'=4,'cols'=4,'depth'=2] {'cols'}, use_global_device_ids=true, to_apply=%add | all-reduce | flops 16 | bytes 128
  30.2 0.1 iota_compare_fusion
  30.2 0.1 iota_compare_fusion.1
  30.3 63.0 %all-gather.5.cloned.1.call-done = bf16[1,16,1,64,2048]{4,3,2,0,1:T(8,128)(2,1)} async-done(((bf16[1,4,1,64,2048]{4,3,2,0,1:T(8,128)(2,1)}), bf16[1,16,1,64,2048]{4,3,2,0,1:T(8,128)(2,1)}) %all-gather.5.cloned.1.call-update) | async-done | bytes 4194320 | tf_op jit(solution)/shard_map/all_gather | solution.py:175
  93.3 53.0 %all-gather.7.cloned.1.call-done = bf16[1,16,1,64,2048]{4,3,2,0,1:T(8,128)(2,1)} async-done(((bf16[1,4,1,64,2048]{4,3,2,0,1:T(8,128)(2,1)}), bf16[1,16,1,64,2048]{4,3,2,0,1:T(8,128)(2,1)}) %all-gather.7.cloned.1.call-update) | async-done | bytes 4194320 | tf_op jit(solution)/shard_map/all_gather | solution.py:178
  146.3 4.7 %fusion.8 = bf16[16,64,64]{2,1,0:T(8,128)(2,1)S(1)} fusion(bf16[1,16,1,64,2048]{4,3,2,0,1:T(8,128)(2,1)} %all-gather.7.cloned.1.call-done, bf16[1,16,1,64,2048]{4,3,2,0,1:T(8,128)(2,1)} %all-gather.5.cloned.1.call-done, pred[16,64]{1,0:T(8,128)(4,1)S(1)} %iota_compare_fusion, pred[16,64]{1,0:T(8,128)(4,1)S(1)} %iota_compare_fusion.1), kind=kOutput, calls=%fused_computation.4 | convolution fusion | flops 268632064 | bytes 8521728 | tf_op jit(solution)/shard_map/kan,kbn->kab/dot_general | solution.py:183
  151.0 0.9 pad_maximum_fusion.refs_3_
  151.9 76.8 %all-gather.9.cloned.1.call-done = bf16[1,16,1,64,2048]{4,3,2,0,1:T(8,128)(2,1)} async-done(((bf16[1,4,1,64,2048]{4,3,2,0,1:T(8,128)(2,1)}), bf16[1,16,1,64,2048]{4,3,2,0,1:T(8,128)(2,1)}) %all-gather.9.cloned.1.call-update) | async-done | bytes 4194320 | tf_op jit(solution)/shard_map/all_gather | solution.py:175
  228.7 53.0 %all-gather.11.cloned.1.call-done = bf16[1,16,1,64,2048]{4,3,2,0,1:T(8,128)(2,1)} async-done(((bf16[1,4,1,64,2048]{4,3,2,0,1:T(8,128)(2,1)}), bf16[1,16,1,64,2048]{4,3,2,0,1:T(8,128)(2,1)}) %all-gather.11.cloned.1.call-update) | async-done | bytes 4194320 | tf_op jit(solution)/shard_map/all_gather | solution.py:178
  281.6 22.5 %layer.1.refs_1_ = f32[2,64,2048]{2,1,0:T(8,128)} custom-call(s32[6]{0:T(128)} %bitcast.38, f32[64,2048]{1,0:T(8,128)} %bitcast.36, f32[64,2048]{1,0:T(8,128)} %bitcast.37, bf16[16,64,128]{2,1,0:T(8,128)(2,1)} %pad_maximum_fusion.refs_3_, bf16[128,2048]{1,0:T(8,128)(2,1)} %constant.8.clone.refs_4_.refs_3_, bf16[16,64,2048]{2,1,0:T(8,128)(2,1)} %bitcast.30, ...), custom_call_target="tpu_custom_call" | custom-call | tf_op jit(solution)/shard_map/layer/pallas_call | solution.py:203
  304.2 0.1 collective-permute-start
  304.3 2.9 collective-permute-done.refs_2_
  307.1 0.0 copy-start
  307.1 1.0 copy-done
  308.1 16.9 %join.1 = (f32[1,1,64,1024]{3,2,1,0:T(8,128)}, f32[1,1,64,1024]{3,2,1,0:T(8,128)}) custom-call(s32[1]{0:T(128)} %bitcast.refs_0_, f32[2,64,2048]{2,1,0:T(8,128)} %layer.1.refs_1_, f32[2,64,2048]{2,1,0:T(8,128)} %copy-done, bf16[128,2048]{1,0:T(8,128)(2,1)} %constant.8.clone.refs_4_.refs_3_), custom_call_target="tpu_custom_call" | custom-call | tf_op jit(solution)/shard_map/join/pallas_call | solution.py:220
  (2 shorter events, 0.0 us)
Async XLA Ops:
  7.2 2.9 copy-start.4
  7.2 13.0 %copy-start.3 = (u32[32]{0:T(128)S(1)}, u32[32]{0:T(128)}, u32[]{:S(2)}) copy-start(u32[32]{0:T(128)} %constant.20) | copy-start | bytes 388
  7.2 4.1 %copy-start.1 = (s32[1,4,1]{1,2,0:T(1,128)S(1)}, s32[1,4,1]{1,2,0:T(1,128)}, u32[]{:S(2)}) copy-start(s32[1,4,1]{1,2,0:T(1,128)} %param.17) | copy-start | bytes 52
  7.2 14.3 %copy-start.2 = (s32[1,4,1]{1,2,0:T(1,128)S(1)}, s32[1,4,1]{1,2,0:T(1,128)}, u32[]{:S(2)}) copy-start(s32[1,4,1]{1,2,0:T(1,128)} %param.14) | copy-start | bytes 52
  7.2 86.1 %all-gather.5.cloned.1.call-start = ((), (), s32[]{:S(2)}) async-start(), calls=%async_computation | async-start | bytes 5242880 | tf_op jit(solution)/shard_map/all_gather | solution.py:175
  7.9 138.4 %all-gather.7.cloned.1.call-start = ((), (), s32[]{:S(2)}) async-start(), calls=%async_computation.1 | async-start | bytes 5242880 | tf_op jit(solution)/shard_map/all_gather | solution.py:178
  8.7 220.0 %all-gather.9.cloned.1.call-start = ((), (), s32[]{:S(2)}) async-start(), calls=%async_computation.2 | async-start | bytes 5242880 | tf_op jit(solution)/shard_map/all_gather | solution.py:175
  9.4 272.2 %all-gather.11.cloned.1.call-start = ((), (), s32[]{:S(2)}) async-start(), calls=%async_computation.3 | async-start | bytes 5242880 | tf_op jit(solution)/shard_map/all_gather | solution.py:178
  304.2 2.9 collective-permute-start
  307.1 1.0 copy-start
Sparse Core Ops, SparseCore 0:
  9.6 83.6 all-gather.4
  95.1 51.1 all-gather.6
  147.9 80.7 all-gather.8
  230.4 51.2 all-gather.10
where the time goes:
time: 332 us; the launch traced here: 331 us
  waiting for transfers between devices  251 us (76%)
  Pallas kernels  39.4 us (12%)
  blocking collectives  17.4 us (5%)
  between operations  15.2 us (5%)
  matrix products  4.7 us (1%)
    all_gather x2, waiting for transfers between devices, gathered(): lax.all_gather(x, 'cols', axis=1, tiled=True)[0, :, 0]  140 us
    all_gather x2, waiting for transfers between devices, gathered(): lax.all_gather(x, 'rows', axis=1, tiled=True)[0, :, 0]  106 us
    pallas_call x1, Pallas kernels, shards(): pl.pallas_call(lambda *refs: layer_kernel(layers, *refs), out_shape=jax.S...  22.5 us
    unnamed x2, blocking collectives  17.4 us
    pallas_call x1, Pallas kernels, shards(): pl.pallas_call(lambda *refs: join_kernel(share, *refs), out_shape=(out, o...  16.9 us
  transfers between devices with their start and end apart: 5, of which 5 were waited for; matrix products, arithmetic and copies ran while one was open for 2% of the time, Pallas kernels for 0%

commit v1 on v0

--- a/solution.py
+++ b/solution.py
@@ -188,12 +188,222 @@
     return row_u, col_u, jnp.concatenate([inner, inner], axis=2)
 
 
+MESH = pl.DeviceIdType.MESH
+
+
+def panels_kernel(n_r, n_c, lu, lv, ru, rv, lu_all, ru_all, inner_all, lv_in, rv_in, own,
+                  local_sem, rv_send, rv_recv, lv_send, lv_recv, lu_send, lu_recv,
+                  ru_send, ru_recv, right_send, left_send, in_send, in_recv):
+    r = lax.axis_index("rows")
+    c = lax.axis_index("cols")
+    d = lax.axis_index("depth")
+    total = n_r * n_c
+    flat = r * n_c + c
+    panel = c * n_r + r
+    rank = lv.shape[1]
+
+    def remote(src, dst, send, recv, row, col):
+        return pltpu.make_async_remote_copy(
+            src_ref=src, dst_ref=dst, send_sem=send, recv_sem=recv,
+            device_id=(row, col, d), device_id_type=MESH)
+
+    def arrived(dst, send, recv):
+        remote(dst, dst, send, recv, lax.rem(r + 1, n_r), c).wait_recv()
+
+    barrier = pltpu.get_barrier_semaphore()
+    for t in range(1, total):
+        to = lax.rem(flat + t, total)
+        pl.semaphore_signal(barrier, inc=1, device_id=(to // n_c, lax.rem(to, n_c), d),
+                            device_id_type=MESH)
+    pl.semaphore_wait(barrier, total - 1)
+
+    rv_self = r == c
+
+    def rv_copy(m):
+        return remote(rv.at[m], rv_in.at[c], rv_send.at[m], rv_recv.at[c], m, r)
+
+    def lv_copy(t):
+        to = lax.rem(r + t, n_r)
+        return remote(lv.at[to], lv_in.at[r], lv_send.at[t], lv_recv.at[r], to, c)
+
+    def lu_copy(side):
+        return remote(lu, lu_all.at[c], lu_send.at[side], lu_recv.at[c], r, c + (1 if side else -1))
+
+    def ru_copy(t):
+        return remote(ru, ru_all.at[r], ru_send.at[t], ru_recv.at[r], lax.rem(r + t, n_r), c)
+
+    for m in range(n_r):
+        @pl.when(jnp.logical_not(jnp.logical_and(rv_self, r == m)))
+        def _():
+            rv_copy(m).start()
+
+    own_rv = pltpu.make_async_copy(rv.at[r], rv_in.at[c], local_sem.at[0])
+    own_lv = pltpu.make_async_copy(lv.at[r], lv_in.at[r], local_sem.at[1])
+    own_lu = pltpu.make_async_copy(lu, lu_all.at[c], local_sem.at[2])
+    own_ru = pltpu.make_async_copy(ru, ru_all.at[r], local_sem.at[3])
+    for t in range(1, n_r):
+        lv_copy(t).start()
+
+    @pl.when(c + 1 < n_c)
+    def _():
+        lu_copy(1).start()
+
+    @pl.when(c > 0)
+    def _():
+        lu_copy(0).start()
+
+    for t in range(1, n_r):
+        ru_copy(t).start()
+
+    @pl.when(rv_self)
+    def _():
+        own_rv.start()
+
+    own_lv.start()
+    own_lu.start()
+    own_ru.start()
+
+    def pass_right(t):
+        s = c - t
+        return remote(lu_all.at[s], lu_all.at[s], right_send.at[t], lu_recv.at[s], r, c + 1)
+
+    def pass_left(t):
+        s = c + t
+        return remote(lu_all.at[s], lu_all.at[s], left_send.at[t], lu_recv.at[s], r, c - 1)
+
+    def relay(t):
+        @pl.when(c - t >= 0)
+        def _():
+            arrived(lu_all.at[c - t], right_send.at[t], lu_recv.at[c - t])
+
+            @pl.when(c + 1 < n_c)
+            def _():
+                pass_right(t).start()
+
+        @pl.when(c + t < n_c)
+        def _():
+            arrived(lu_all.at[c + t], left_send.at[t], lu_recv.at[c + t])
+
+            @pl.when(c > 0)
+            def _():
+                pass_left(t).start()
+
+    relay(1)
+    for j in range(n_c):
+        @pl.when(jnp.logical_not(jnp.logical_and(rv_self, c == j)))
+        def _():
+            arrived(rv_in.at[j], rv_send.at[0], rv_recv.at[j])
+
+    @pl.when(rv_self)
+    def _():
+        own_rv.wait()
+
+    own_lv.wait()
+    for t in range(1, n_r):
+        source = lax.rem(r + t, n_r)
+        arrived(lv_in.at[source], lv_send.at[t], lv_recv.at[source])
+    lefts = lv_in[...].reshape(n_r * rank, lv_in.shape[2])
+    for j in range(n_c):
+        right = rv_in[j]
+        both = jnp.concatenate([right, right], axis=0)
+        inner = dot(lefts, both, (1, 1), None).astype(jnp.bfloat16)
+        own[j] = inner.reshape(n_r, rank, 2 * rank)
+
+    def in_copy(t):
+        to = lax.rem(flat + t, total)
+        row = to // n_c
+        col = lax.rem(to, n_c)
+        return remote(own.at[col, row], inner_all.at[panel], in_send.at[t], in_recv.at[panel], row, col)
+
+    for t in range(1, total):
+        in_copy(t).start()
+    own_inner = pltpu.make_async_copy(own.at[c, r], inner_all.at[panel], local_sem.at[4])
+    own_inner.start()
+    for t in range(2, n_c):
+        relay(t)
+    for t in range(1, n_r):
+        source = lax.rem(r + t, n_r)
+        arrived(ru_all.at[source], ru_send.at[t], ru_recv.at[source])
+    for t in range(1, total):
+        source = lax.rem(panel + t, total)
+        arrived(inner_all.at[source], in_send.at[t], in_recv.at[source])
+    own_inner.wait()
+    own_lu.wait()
+    own_ru.wait()
+    for m in range(n_r):
+        @pl.when(jnp.logical_not(jnp.logical_and(rv_self, r == m)))
+        def _():
+            rv_copy(m).wait_send()
+    for t in range(1, n_r):
+        lv_copy(t).wait_send()
+        ru_copy(t).wait_send()
+
+    @pl.when(c + 1 < n_c)
+    def _():
+        lu_copy(1).wait_send()
+
+    @pl.when(c > 0)
+    def _():
+        lu_copy(0).wait_send()
+
+    for t in range(1, n_c):
+        @pl.when(jnp.logical_and(c - t >= 0, c + 1 < n_c))
+        def _():
+            pass_right(t).wait_send()
+
+        @pl.when(jnp.logical_and(c + t < n_c, c > 0))
+        def _():
+            pass_left(t).wait_send()
+    for t in range(1, total):
+        in_copy(t).wait_send()
+
+
+def exchanged(left_u, left_v, rank_left, right_u, right_v, rank_right):
+    n_r = lax.axis_size("rows")
+    n_c = lax.axis_size("cols")
+    lu, lv, rl = (x[0, :, 0] for x in (left_u, left_v, rank_left))
+    ru, rv, rr = (x[0, :, 0] for x in (right_u, right_v, rank_right))
+    rank, width = lu.shape[1:]
+    index = jnp.arange(rank)
+    lv = jnp.where((index[None, :] < rl[:, None])[:, :, None], lv, 0)
+    rv = jnp.where((index[None, :] < rr[:, None])[:, :, None], rv, 0)
+    hbm = pl.BlockSpec(memory_space=pl.ANY)
+    total = n_r * n_c
+    bf16 = jnp.bfloat16
+    dma = pltpu.SemaphoreType.DMA
+    lu_all, ru_all, inner = pl.pallas_call(
+        lambda *refs: panels_kernel(n_r, n_c, *refs),
+        out_shape=(
+            jax.ShapeDtypeStruct((n_c,) + lu.shape, bf16),
+            jax.ShapeDtypeStruct((n_r,) + ru.shape, bf16),
+            jax.ShapeDtypeStruct((total, rank, 2 * rank), bf16),
+        ),
+        in_specs=[hbm] * 4,
+        out_specs=(hbm, hbm, hbm),
+        scratch_shapes=[
+            pltpu.VMEM((n_r, rank, width), bf16),
+            pltpu.VMEM((n_c, rank, width), bf16),
+            pltpu.VMEM((n_c, n_r, rank, 2 * rank), bf16),
+            dma((5,)),
+            dma((n_r,)), dma((n_c,)), dma((n_r,)), dma((n_r,)),
+            dma((2,)), dma((n_c,)), dma((n_r,)), dma((n_r,)),
+            dma((n_c,)), dma((n_c,)), dma((total,)), dma((total,)),
+        ],
+        compiler_params=pltpu.CompilerParams(
+            collective_id=0, has_side_effects=True, vmem_limit_bytes=56 * 2**20),
+        name="panels",
+    )(lu, lv, ru, rv)
+    return (lu_all.reshape(total, rank, width), ru_all.reshape(total, rank, width), inner)
+
+
 def shards(tile_left, tile_right, left_u, left_v, rank_left, right_u, right_v, rank_right, triples):
     layers = lax.axis_size("depth")
     rank, width = tile_left.shape[2:]
     slots = triples.shape[3]
     share = width // layers
-    row_u, col_u, inner = gathered(left_u, left_v, rank_left, right_u, right_v, rank_right)
+    sizes = {lax.axis_size("rows"), lax.axis_size("cols"), left_u.shape[1], right_u.shape[1]}
+    bring = exchanged if len(sizes) == 1 else gathered
+    row_u, col_u, inner = bring(left_u, left_v, rank_left, right_u, right_v, rank_right)
     table = jnp.asarray(start_table(rank, width))
     smem = pl.BlockSpec(memory_space=pltpu.SMEM)
     vmem = pl.BlockSpec(memory_space=pltpu.VMEM)

time: 332 us -> 197 us (0.59)
  waiting for transfers between devices: 251 us -> 2.85 us
  Pallas kernels: 39.4 us -> 188 us
  blocking collectives: 17.4 us -> 0 us
  between operations: 15.2 us -> 0.66 us
  matrix products: 4.7 us -> 0 us
  other arithmetic: 1 us -> 4.57 us
    all_gather x4 -> x0, waiting for transfers between devices: 246 us -> none  [the longest x2 140 us: gathered(): lax.all_gather(x, 'cols', axis=1, tiled=True)[0, :, 0]]
    pallas_call x0 -> x1, Pallas kernels: none -> 149 us  [exchanged(): pl.pallas_call(lambda *refs: panels_kernel(n_r, n_c, *refs), out_shape=(j...]
    unnamed x2 -> x0, blocking collectives: 17.4 us -> none
    dot_general x1 -> x0, matrix products: 4.7 us -> none  [gathered(): jnp.einsum('kan,kbn->kab', row_v, col_v, preferred_element_type=jnp.float32)]
  transfers between devices with their start and end apart: 5 -> 1, of which waited for: 5 -> 1; matrix products, arithmetic and copies ran while one was open for 2% -> 0% of each run, Pallas kernels for 0% -> 0%
where the time goes in v1:
time: 197 us
  Pallas kernels  188 us (95%)
  other arithmetic  4.57 us (2%)
  waiting for transfers between devices  2.85 us (1%)
    pallas_call x1, Pallas kernels, exchanged(): pl.pallas_call(lambda *refs: panels_kernel(n_r, n_c, *refs), out_shape=(j...  149 us
    pallas_call x1, Pallas kernels, shards(): pl.pallas_call(lambda *refs: layer_kernel(layers, *refs), out_shape=jax.S...  22.7 us
    pallas_call x1, Pallas kernels, shards(): pl.pallas_call(lambda *refs: join_kernel(share, *refs), out_shape=(out, o...  16.9 us
  transfers between devices with their start and end apart: 1, of which 1 were waited for; matrix products, arithmetic and copies ran while one was open for 0% of the time, Pallas kernels for 0%

profile of v1, /device:TPU:0, one launch (start us, length us, event | category | flops | bytes accessed | tf_op | source)
XLA Modules:
  0.0 197.2 jit_solution(4397475619413590748)
XLA Ops:
  0.6 0.7 iota_compare_fusion
  1.4 0.7 iota_compare_fusion.1
  2.1 3.1 %bitcast_select_fusion = (bf16[4,64,2048]{2,1,0:T(8,128)(2,1)}, bf16[4,64,2048]{2,1,0:T(8,128)(2,1)}) fusion(bf16[1,4,1,64,2048]{4,3,2,1,0:T(8,128)(2,1)} %param.16, pred[4,64]{1,0:T(4,128)(4,1)S(1)} %iota_compare_fusion, bf16[1,4,1,64,2048]{4,3,2,1,0:T(8,128)(2,1)} %param.13, pred[4,64]{1,0:T(4,128)(4,1)S(1)} %iota_compare_fusion.1), kind=kLoop, calls=%fused_computation | loop fusion | flops 1048576 | bytes 4194816 | tf_op jit(solution)/shard_map/jit(_where)/select_n | solution.py:369
  5.2 148.6 %panels.1 = (bf16[4,4,64,2048]{3,2,1,0:T(8,128)(2,1)}, bf16[4,4,64,2048]{3,2,1,0:T(8,128)(2,1)}, bf16[16,64,128]{2,1,0:T(8,128)(2,1)}) custom-call(bf16[4,64,2048]{2,1,0:T(8,128)(2,1)} %bitcast.16, bf16[4,64,2048]{2,1,0:T(8,128)(2,1)} %get-tuple-element.9.refs_1_, bf16[4,64,2048]{2,1,0:T(8,128)(2,1)} %bitcast.17, bf16[4,64,2048]{2,1,0:T(8,128)(2,1)} %get-tuple-element.8.refs_3_), custom_call_target="tpu_custom_call" | custom-call | tf_op jit(solution)/shard_map/panels/pallas_call | solution.py:374
  153.8 22.7 %layer.1.refs_1_ = f32[2,64,2048]{2,1,0:T(8,128)} custom-call(s32[6]{0:T(128)} %bitcast.20, f32[64,2048]{1,0:T(8,128)} %bitcast.18, f32[64,2048]{1,0:T(8,128)} %bitcast.19, bf16[16,64,128]{2,1,0:T(8,128)(2,1)} %get-tuple-element.5.refs_3_, bf16[128,2048]{1,0:T(8,128)(2,1)} %constant.9.clone.refs_4_.refs_3_, bf16[16,64,2048]{2,1,0:T(8,128)(2,1)} %bitcast.14, ...), custom_call_target="tpu_custom_call" | custom-call | tf_op jit(solution)/shard_map/layer/pallas_call | solution.py:413
  176.4 0.1 collective-permute-start
  176.5 2.9 %collective-permute-done.refs_2_ = f32[2,64,2048]{2,1,0:T(8,128)S(1)} collective-permute-done((f32[2,64,2048]{2,1,0:T(8,128)}, f32[2,64,2048]{2,1,0:T(8,128)S(1)}, u32[]{:S(2)}, u32[]{:S(2)}) %collective-permute-start) | collective-permute-done | bytes 1048608 | tf_op jit(solution)/shard_map/ppermute | solution.py:427
  179.4 0.0 copy-start
  179.4 1.0 copy-done
  180.3 16.9 %join.1 = (f32[1,1,64,1024]{3,2,1,0:T(8,128)}, f32[1,1,64,1024]{3,2,1,0:T(8,128)}) custom-call(s32[1]{0:T(128)} %bitcast.refs_0_, f32[2,64,2048]{2,1,0:T(8,128)} %layer.1.refs_1_, f32[2,64,2048]{2,1,0:T(8,128)} %copy-done, bf16[128,2048]{1,0:T(8,128)(2,1)} %constant.9.clone.refs_4_.refs_3_), custom_call_target="tpu_custom_call" | custom-call | tf_op jit(solution)/shard_map/join/pallas_call | solution.py:430
Async XLA Ops:
  176.4 2.9 %collective-permute-start = (f32[2,64,2048]{2,1,0:T(8,128)}, f32[2,64,2048]{2,1,0:T(8,128)S(1)}, u32[]{:S(2)}, u32[]{:S(2)}) collective-permute-start(f32[2,64,2048]{2,1,0:T(8,128)} %layer.1.refs_1_), channel_id=1, source_target_pairs={{0,1},{1,0},{2,3},{3,2},{4,5},{5,4},{6,7},{7,6},{8,9},{9,8},{10,11... | collective-permute-start | bytes 3145736 | tf_op jit(solution)/shard_map/ppermute | solution.py:427
  179.4 1.0 copy-start

commit v2 on v1

--- a/solution.py
+++ b/solution.py
@@ -36,6 +36,25 @@
 def split(value):
     high = value.astype(jnp.bfloat16)
     return high, (value - high.astype(jnp.float32)).astype(jnp.bfloat16)
+
+
+def thirds(value):
+    first, rest = value.astype(jnp.bfloat16), value
+    rest = rest - first.astype(jnp.float32)
+    second = rest.astype(jnp.bfloat16)
+    return first, second, (rest - second.astype(jnp.float32)).astype(jnp.bfloat16)
+
+
+def dot_pieces(value, pieces):
+    rows = value.shape[0]
+    parts = thirds(value)
+    total = None
+    for index in (2, 1, 0):
+        both = dot(jnp.concatenate(parts[: 3 - index], axis=0), pieces[index], (1, 0), None)
+        for part in reversed(range(3 - index)):
+            term = both[rows * part : rows * (part + 1)]
+            total = term if total is None else total + term
+    return total
 
 
 def inverse_factor(image, coeff):
@@ -83,10 +102,10 @@
 def sweeps(seen, gram_left, gram_right, to_right, to_left):
     for _ in range(2):
         coeff = to_right(seen)
-        image = dot(coeff, gram_right)
+        image = dot_pieces(coeff, gram_right)
         seen = dot(inverse_factor(image, coeff), image)
         coeff = to_left(seen)
-        image = dot(coeff, gram_left)
+        image = dot_pieces(coeff, gram_left)
         inverse = inverse_factor(image, coeff)
         seen = dot(inverse, image)
     return dot(inverse, coeff), to_right(seen)
@@ -124,8 +143,8 @@
         copy.wait()
     left = xs[...]
     right = ys[...]
-    gram_left = dot(left, left, (1, 1), None)
-    gram_right = dot(right, right, (1, 1), None)
+    gram_left = thirds(dot(left, left, (1, 1), None))
+    gram_right = thirds(dot(right, right, (1, 1), None))
     seen = dot(table[...], left, (1, 1), None)
     seen = seen[:rank] + seen[rank:]
     pairs = kmat.shape[0]
@@ -151,23 +170,33 @@
     rank = mine.shape[1]
     width = mine.shape[2]
     is_upper = upper[0] == 1
+    both = 2 * rank
     stacks = []
     for index in range(2):
         a, b = mine[index], other[index]
-        stacks.append(
-            jnp.concatenate([jnp.where(is_upper, b, a), jnp.where(is_upper, a, b)], axis=0)
-        )
+        value = jnp.concatenate([jnp.where(is_upper, b, a), jnp.where(is_upper, a, b)], axis=0)
+        stacks.append(jnp.concatenate(split(value), axis=0))
     left, right = stacks
-    gram_left = dot(left, left, (1, 1))
-    gram_right = dot(right, right, (1, 1))
-    start = table[pl.ds(0, rank)].astype(jnp.float32) + table[pl.ds(rank, rank)].astype(jnp.float32)
-    seen = dot(start, left, (1, 1))
-    probe, image = sweeps(seen, gram_left, gram_right, lambda v: v, lambda v: v)
+
+    def folded(stack):
+        gram = dot(stack, stack, (1, 1), None)
+        gram = gram[:both] + gram[both:]
+        return thirds(gram[:, :both] + gram[:, both:])
+
+    seen = dot(table[...], left, (1, 1), None)
+    seen = seen[:rank] + seen[rank:]
+    seen = seen[:, :both] + seen[:, both:]
+    probe, image = sweeps(seen, folded(left), folded(right), lambda v: v, lambda v: v)
     scale = math.sqrt(width)
-    left = jnp.where(is_upper, left[:, share:], left[:, :share])
-    right = jnp.where(is_upper, right[:, share:], right[:, :share])
-    new_left[0, 0] = dot(probe, left) * scale
-    new_right[0, 0] = dot(image, right) / scale
+
+    def expand(coeff, stack):
+        pieces = jnp.concatenate(split(coeff), axis=0)
+        half = jnp.where(is_upper, stack[:, share:], stack[:, :share])
+        out = dot(jnp.concatenate([pieces, pieces], axis=1), half, (1, 0), None)
+        return out[:rank] + out[rank:]
+
+    new_left[0, 0] = expand(probe, left) * scale
+    new_right[0, 0] = expand(image, right) / scale
 
 
 def gathered(left_u, left_v, rank_left, right_u, right_v, rank_right):
@@ -227,10 +256,24 @@
         return remote(lv.at[to], lv_in.at[r], lv_send.at[t], lv_recv.at[r], to, c)
 
     def lu_copy(side):
-        return remote(lu, lu_all.at[c], lu_send.at[side], lu_recv.at[c], r, c + (1 if side else -1))
+        return [
+            remote(lu.at[q], lu_all.at[c, q], lu_send.at[side, q], lu_recv.at[c, q], r,
+                   c + (1 if side else -1))
+            for q in range(lu.shape[0])
+        ]
 
     def ru_copy(t):
         return remote(ru, ru_all.at[r], ru_send.at[t], ru_recv.at[r], lax.rem(r + t, n_r), c)
+
+    @pl.when(c + 1 < n_c)
+    def _():
+        for copy in lu_copy(1):
+            copy.start()
+
+    @pl.when(c > 0)
+    def _():
+        for copy in lu_copy(0):
+            copy.start()
 
     for m in range(n_r):
         @pl.when(jnp.logical_not(jnp.logical_and(rv_self, r == m)))
@@ -244,14 +287,6 @@
     for t in range(1, n_r):
         lv_copy(t).start()
 
-    @pl.when(c + 1 < n_c)
-    def _():
-        lu_copy(1).start()
-
-    @pl.when(c > 0)
-    def _():
-        lu_copy(0).start()
-
     for t in range(1, n_r):
         ru_copy(t).start()
 
@@ -263,32 +298,37 @@
     own_lu.start()
     own_ru.start()
 
-    def pass_right(t):
+    def pass_right(t, q):
         s = c - t
-        return remote(lu_all.at[s], lu_all.at[s], right_send.at[t], lu_recv.at[s], r, c + 1)
-
-    def pass_left(t):
+        return remote(lu_all.at[s, q], lu_all.at[s, q], right_send.at[t, q], lu_recv.at[s, q], r, c + 1)
+
+    def pass_left(t, q):
         s = c + t
-        return remote(lu_all.at[s], lu_all.at[s], left_send.at[t], lu_recv.at[s], r, c - 1)
-
-    def relay(t):
+        return remote(lu_all.at[s, q], lu_all.at[s, q], left_send.at[t, q], lu_recv.at[s, q], r, c - 1)
+
+    def relay_one(t, q):
         @pl.when(c - t >= 0)
         def _():
-            arrived(lu_all.at[c - t], right_send.at[t], lu_recv.at[c - t])
+            arrived(lu_all.at[c - t, q], right_send.at[t, q], lu_recv.at[c - t, q])
 
             @pl.when(c + 1 < n_c)
             def _():
-                pass_right(t).start()
+                pass_right(t, q).start()
 
         @pl.when(c + t < n_c)
         def _():
-            arrived(lu_all.at[c + t], left_send.at[t], lu_recv.at[c + t])
+            arrived(lu_all.at[c + t, q], left_send.at[t, q], lu_recv.at[c + t, q])
 
             @pl.when(c > 0)
             def _():
-                pass_left(t).start()
-
-    relay(1)
+                pass_left(t, q).start()
+
+    def relay(t):
+        for q in range(lu.shape[0]):
+            relay_one(t, q)
+
+    for t in range(1, n_c - 1):
+        relay(t)
     for j in range(n_c):
         @pl.when(jnp.logical_not(jnp.logical_and(rv_self, c == j)))
         def _():
@@ -319,8 +359,7 @@
         in_copy(t).start()
     own_inner = pltpu.make_async_copy(own.at[c, r], inner_all.at[panel], local_sem.at[4])
     own_inner.start()
-    for t in range(2, n_c):
-        relay(t)
+    relay(n_c - 1)
     for t in range(1, n_r):
         source = lax.rem(r + t, n_r)
         arrived(ru_all.at[source], ru_send.at[t], ru_recv.at[source])
@@ -340,20 +379,24 @@
 
     @pl.when(c + 1 < n_c)
     def _():
-        lu_copy(1).wait_send()
+        for copy in lu_copy(1):
+            copy.wait_send()
 
     @pl.when(c > 0)
     def _():
-        lu_copy(0).wait_send()
+        for copy in lu_copy(0):
+            copy.wait_send()
 
     for t in range(1, n_c):
         @pl.when(jnp.logical_and(c - t >= 0, c + 1 < n_c))
         def _():
-            pass_right(t).wait_send()
+            for q in range(lu.shape[0]):
+                pass_right(t, q).wait_send()
 
         @pl.when(jnp.logical_and(c + t < n_c, c > 0))
         def _():
-            pass_left(t).wait_send()
+            for q in range(lu.shape[0]):
+                pass_left(t, q).wait_send()
     for t in range(1, total):
         in_copy(t).wait_send()
 
@@ -369,6 +412,7 @@
     rv = jnp.where((index[None, :] < rr[:, None])[:, :, None], rv, 0)
     hbm = pl.BlockSpec(memory_space=pl.ANY)
     total = n_r * n_c
+    per = lu.shape[0]
     bf16 = jnp.bfloat16
     dma = pltpu.SemaphoreType.DMA
     lu_all, ru_all, inner = pl.pallas_call(
@@ -386,8 +430,8 @@
             pltpu.VMEM((n_c, n_r, rank, 2 * rank), bf16),
             dma((5,)),
             dma((n_r,)), dma((n_c,)), dma((n_r,)), dma((n_r,)),
-            dma((2,)), dma((n_c,)), dma((n_r,)), dma((n_r,)),
-            dma((n_c,)), dma((n_c,)), dma((total,)), dma((total,)),
+            dma((2, per)), dma((n_c, per)), dma((n_r,)), dma((n_r,)),
+            dma((n_c, per)), dma((n_c, per)), dma((total,)), dma((total,)),
         ],
         compiler_params=pltpu.CompilerParams(
             collective_id=0, has_side_effects=True, vmem_limit_bytes=56 * 2**20),

time: 197 us -> 195 us (0.990)
  Pallas kernels: 188 us -> 185 us
    pallas_call x1, Pallas kernels: 16.9 us -> 14.1 us  [shards(): pl.pallas_call(lambda *refs: join_kernel(share, *refs), out_shape=(out, o...]
where the time goes in v2:
time: 195 us; the launch traced here: 194 us
  Pallas kernels  185 us (95%)
  other arithmetic  4.57 us (2%)
  waiting for transfers between devices  2.85 us (1%)
    pallas_call x1, Pallas kernels, exchanged(): pl.pallas_call(lambda *refs: panels_kernel(n_r, n_c, *refs), out_shape=(j...  149 us
    pallas_call x1, Pallas kernels, shards(): pl.pallas_call(lambda *refs: layer_kernel(layers, *refs), out_shape=jax.S...  22.4 us
    pallas_call x1, Pallas kernels, shards(): pl.pallas_call(lambda *refs: join_kernel(share, *refs), out_shape=(out, o...  14.1 us
  transfers between devices with their start and end apart: 1, of which 1 were waited for; matrix products, arithmetic and copies ran while one was open for 0% of the time, Pallas kernels for 0%

profile of v2, /device:TPU:0, one launch (start us, length us, event | category | flops | bytes accessed | tf_op | source)
XLA Modules:
  0.0 194.4 jit_solution(15697456871094661520)
XLA Ops:
  0.6 0.7 iota_compare_fusion
  1.4 0.7 iota_compare_fusion.1
  2.1 3.1 %bitcast_select_fusion = (bf16[4,64,2048]{2,1,0:T(8,128)(2,1)}, bf16[4,64,2048]{2,1,0:T(8,128)(2,1)}) fusion(bf16[1,4,1,64,2048]{4,3,2,1,0:T(8,128)(2,1)} %param.16, pred[4,64]{1,0:T(4,128)(4,1)S(1)} %iota_compare_fusion, bf16[1,4,1,64,2048]{4,3,2,1,0:T(8,128)(2,1)} %param.13, pred[4,64]{1,0:T(4,128)(4,1)S(1)} %iota_compare_fusion.1), kind=kLoop, calls=%fused_computation | loop fusion | flops 1048576 | bytes 4194816 | tf_op jit(solution)/shard_map/jit(_where)/select_n | solution.py:412
  5.2 148.8 %panels.1 = (bf16[4,4,64,2048]{3,2,1,0:T(8,128)(2,1)}, bf16[4,4,64,2048]{3,2,1,0:T(8,128)(2,1)}, bf16[16,64,128]{2,1,0:T(8,128)(2,1)}) custom-call(bf16[4,64,2048]{2,1,0:T(8,128)(2,1)} %bitcast.16, bf16[4,64,2048]{2,1,0:T(8,128)(2,1)} %get-tuple-element.9.refs_1_, bf16[4,64,2048]{2,1,0:T(8,128)(2,1)} %bitcast.17, bf16[4,64,2048]{2,1,0:T(8,128)(2,1)} %get-tuple-element.8.refs_3_), custom_call_target="tpu_custom_call" | custom-call | tf_op jit(solution)/shard_map/panels/pallas_call | solution.py:418
  154.0 22.4 %layer.1.refs_1_ = f32[2,64,2048]{2,1,0:T(8,128)} custom-call(s32[6]{0:T(128)} %bitcast.20, f32[64,2048]{1,0:T(8,128)} %bitcast.18, f32[64,2048]{1,0:T(8,128)} %bitcast.19, bf16[16,64,128]{2,1,0:T(8,128)(2,1)} %get-tuple-element.5.refs_3_, bf16[128,2048]{1,0:T(8,128)(2,1)} %constant.9.clone.refs_4_.refs_3_, bf16[16,64,2048]{2,1,0:T(8,128)(2,1)} %bitcast.14, ...), custom_call_target="tpu_custom_call" | custom-call | tf_op jit(solution)/shard_map/layer/pallas_call | solution.py:457
  176.4 0.1 collective-permute-start
  176.5 2.9 %collective-permute-done.refs_2_ = f32[2,64,2048]{2,1,0:T(8,128)S(1)} collective-permute-done((f32[2,64,2048]{2,1,0:T(8,128)}, f32[2,64,2048]{2,1,0:T(8,128)S(1)}, u32[]{:S(2)}, u32[]{:S(2)}) %collective-permute-start) | collective-permute-done | bytes 1048608 | tf_op jit(solution)/shard_map/ppermute | solution.py:471
  179.4 0.0 copy-start
  179.4 1.0 copy-done
  180.3 14.1 %join.1 = (f32[1,1,64,1024]{3,2,1,0:T(8,128)}, f32[1,1,64,1024]{3,2,1,0:T(8,128)}) custom-call(s32[1]{0:T(128)} %bitcast.refs_0_, f32[2,64,2048]{2,1,0:T(8,128)} %layer.1.refs_1_, f32[2,64,2048]{2,1,0:T(8,128)} %copy-done, bf16[128,2048]{1,0:T(8,128)(2,1)} %constant.9.clone.refs_4_.refs_3_), custom_call_target="tpu_custom_call" | custom-call | tf_op jit(solution)/shard_map/join/pallas_call | solution.py:474
Async XLA Ops:
  176.4 2.9 %collective-permute-start = (f32[2,64,2048]{2,1,0:T(8,128)}, f32[2,64,2048]{2,1,0:T(8,128)S(1)}, u32[]{:S(2)}, u32[]{:S(2)}) collective-permute-start(f32[2,64,2048]{2,1,0:T(8,128)} %layer.1.refs_1_), channel_id=1, source_target_pairs={{0,1},{1,0},{2,3},{3,2},{4,5},{5,4},{6,7},{7,6},{8,9},{9,8},{10,11... | collective-permute-start | bytes 3145736 | tf_op jit(solution)/shard_map/ppermute | solution.py:471
  179.4 1.0 copy-start

commit v3 on v2

--- a/solution.py
+++ b/solution.py
@@ -220,8 +220,8 @@
 MESH = pl.DeviceIdType.MESH
 
 
-def panels_kernel(n_r, n_c, lu, lv, ru, rv, lu_all, ru_all, inner_all, lv_in, rv_in, own,
-                  local_sem, rv_send, rv_recv, lv_send, lv_recv, lu_send, lu_recv,
+def panels_kernel(n_r, n_c, lu, lv, ru, rv, lu_all, ru_all, inner_all, lv_in, rv_mid, rv_in, own,
+                  local_sem, mid_send, mid_recv, rv_send, rv_recv, lv_send, lv_recv, lu_send, lu_recv,
                   ru_send, ru_recv, right_send, left_send, in_send, in_recv):
     r = lax.axis_index("rows")
     c = lax.axis_index("cols")
@@ -246,10 +246,13 @@
                             device_id_type=MESH)
     pl.semaphore_wait(barrier, total - 1)
 
-    rv_self = r == c
-
-    def rv_copy(m):
-        return remote(rv.at[m], rv_in.at[c], rv_send.at[m], rv_recv.at[c], m, r)
+    def mid_copy(t):
+        to = lax.rem(r + t, n_r)
+        return remote(rv.at[to], rv_mid.at[r], mid_send.at[t], mid_recv.at[r], to, c)
+
+    def rv_copy(t):
+        to = lax.rem(c + t, n_c)
+        return remote(rv_mid.at[to], rv_in.at[c], rv_send.at[t], rv_recv.at[c], r, to)
 
     def lv_copy(t):
         to = lax.rem(r + t, n_r)
@@ -275,12 +278,11 @@
         for copy in lu_copy(0):
             copy.start()
 
-    for m in range(n_r):
-        @pl.when(jnp.logical_not(jnp.logical_and(rv_self, r == m)))
-        def _():
-            rv_copy(m).start()
-
-    own_rv = pltpu.make_async_copy(rv.at[r], rv_in.at[c], local_sem.at[0])
+    for t in range(1, n_r):
+        mid_copy(t).start()
+    own_mid = pltpu.make_async_copy(rv.at[r], rv_mid.at[r], local_sem.at[5])
+    own_mid.start()
+    own_rv = pltpu.make_async_copy(rv_mid.at[c], rv_in.at[c], local_sem.at[0])
     own_lv = pltpu.make_async_copy(lv.at[r], lv_in.at[r], local_sem.at[1])
     own_lu = pltpu.make_async_copy(lu, lu_all.at[c], local_sem.at[2])
     own_ru = pltpu.make_async_copy(ru, ru_all.at[r], local_sem.at[3])
@@ -290,13 +292,16 @@
     for t in range(1, n_r):
         ru_copy(t).start()
 
-    @pl.when(rv_self)
-    def _():
-        own_rv.start()
-
     own_lv.start()
     own_lu.start()
     own_ru.start()
+    own_mid.wait()
+    for t in range(1, n_r):
+        source = lax.rem(r + t, n_r)
+        arrived(rv_mid.at[source], mid_send.at[t], mid_recv.at[source])
+    for t in range(1, n_c):
+        rv_copy(t).start()
+    own_rv.start()
 
     def pass_right(t, q):
         s = c - t
@@ -329,15 +334,10 @@
 
     for t in range(1, n_c - 1):
         relay(t)
-    for j in range(n_c):
-        @pl.when(jnp.logical_not(jnp.logical_and(rv_self, c == j)))
-        def _():
-            arrived(rv_in.at[j], rv_send.at[0], rv_recv.at[j])
-
-    @pl.when(rv_self)
-    def _():
-        own_rv.wait()
-
+    for t in range(1, n_c):
+        source = lax.rem(c + t, n_c)
+        arrived(rv_in.at[source], rv_send.at[t], rv_recv.at[source])
+    own_rv.wait()
     own_lv.wait()
     for t in range(1, n_r):
         source = lax.rem(r + t, n_r)
@@ -369,11 +369,10 @@
     own_inner.wait()
     own_lu.wait()
     own_ru.wait()
-    for m in range(n_r):
-        @pl.when(jnp.logical_not(jnp.logical_and(rv_self, r == m)))
-        def _():
-            rv_copy(m).wait_send()
-    for t in range(1, n_r):
+    for t in range(1, n_c):
+        rv_copy(t).wait_send()
+    for t in range(1, n_r):
+        mid_copy(t).wait_send()
         lv_copy(t).wait_send()
         ru_copy(t).wait_send()
 
@@ -426,10 +425,11 @@
         out_specs=(hbm, hbm, hbm),
         scratch_shapes=[
             pltpu.VMEM((n_r, rank, width), bf16),
+            pltpu.VMEM((n_r, rank, width), bf16),
             pltpu.VMEM((n_c, rank, width), bf16),
             pltpu.VMEM((n_c, n_r, rank, 2 * rank), bf16),
-            dma((5,)),
-            dma((n_r,)), dma((n_c,)), dma((n_r,)), dma((n_r,)),
+            dma((6,)), dma((n_r,)), dma((n_r,)),
+            dma((n_c,)), dma((n_c,)), dma((n_r,)), dma((n_r,)),
             dma((2, per)), dma((n_c, per)), dma((n_r,)), dma((n_r,)),
             dma((n_c, per)), dma((n_c, per)), dma((total,)), dma((total,)),
         ],

time: 195 us -> 144 us (0.74)
  Pallas kernels: 185 us -> 134 us
    pallas_call x1, Pallas kernels: 149 us -> 97.9 us  [exchanged(): pl.pallas_call(lambda *refs: panels_kernel(n_r, n_c, *refs), out_shape=(j...]
where the time goes in v3:
time: 144 us
  Pallas kernels  134 us (93%)
  other arithmetic  4.57 us (3%)
  waiting for transfers between devices  2.85 us (2%)
    pallas_call x1, Pallas kernels, exchanged(): pl.pallas_call(lambda *refs: panels_kernel(n_r, n_c, *refs), out_shape=(j...  97.9 us
    pallas_call x1, Pallas kernels, shards(): pl.pallas_call(lambda *refs: layer_kernel(layers, *refs), out_shape=jax.S...  22.5 us
    pallas_call x1, Pallas kernels, shards(): pl.pallas_call(lambda *refs: join_kernel(share, *refs), out_shape=(out, o...  14.1 us
    select_n x1, other arithmetic, exchanged(): rv = jnp.where((index[None, :] < rr[:, None])[:, :, None], rv, 0)  3.11 us
  transfers between devices with their start and end apart: 1, of which 1 were waited for; matrix products, arithmetic and copies ran while one was open for 0% of the time, Pallas kernels for 0%

profile of v3, /device:TPU:0, one launch (start us, length us, event | category | flops | bytes accessed | tf_op | source)
XLA Modules:
  0.0 143.6 jit_solution(11695975490108428194)
XLA Ops:
  0.6 0.7 iota_compare_fusion
  1.4 0.7 iota_compare_fusion.1
  2.1 3.1 %bitcast_select_fusion = (bf16[4,64,2048]{2,1,0:T(8,128)(2,1)}, bf16[4,64,2048]{2,1,0:T(8,128)(2,1)}) fusion(bf16[1,4,1,64,2048]{4,3,2,1,0:T(8,128)(2,1)} %param.16, pred[4,64]{1,0:T(4,128)(4,1)S(1)} %iota_compare_fusion, bf16[1,4,1,64,2048]{4,3,2,1,0:T(8,128)(2,1)} %param.13, pred[4,64]{1,0:T(4,128)(4,1)S(1)} %iota_compare_fusion.1), kind=kLoop, calls=%fused_computation | loop fusion | flops 1048576 | bytes 4194816 | tf_op jit(solution)/shard_map/jit(_where)/select_n | solution.py:411
  5.2 97.9 %panels.1 = (bf16[4,4,64,2048]{3,2,1,0:T(8,128)(2,1)}, bf16[4,4,64,2048]{3,2,1,0:T(8,128)(2,1)}, bf16[16,64,128]{2,1,0:T(8,128)(2,1)}) custom-call(bf16[4,64,2048]{2,1,0:T(8,128)(2,1)} %bitcast.16, bf16[4,64,2048]{2,1,0:T(8,128)(2,1)} %get-tuple-element.9.refs_1_, bf16[4,64,2048]{2,1,0:T(8,128)(2,1)} %bitcast.17, bf16[4,64,2048]{2,1,0:T(8,128)(2,1)} %get-tuple-element.8.refs_3_), custom_call_target="tpu_custom_call" | custom-call | tf_op jit(solution)/shard_map/panels/pallas_call | solution.py:417
  103.2 22.5 %layer.1.refs_1_ = f32[2,64,2048]{2,1,0:T(8,128)} custom-call(s32[6]{0:T(128)} %bitcast.20, f32[64,2048]{1,0:T(8,128)} %bitcast.18, f32[64,2048]{1,0:T(8,128)} %bitcast.19, bf16[16,64,128]{2,1,0:T(8,128)(2,1)} %get-tuple-element.5.refs_3_, bf16[128,2048]{1,0:T(8,128)(2,1)} %constant.9.clone.refs_4_.refs_3_, bf16[16,64,2048]{2,1,0:T(8,128)(2,1)} %bitcast.14, ...), custom_call_target="tpu_custom_call" | custom-call | tf_op jit(solution)/shard_map/layer/pallas_call | solution.py:457
  125.6 0.1 collective-permute-start
  125.7 2.9 %collective-permute-done.refs_2_ = f32[2,64,2048]{2,1,0:T(8,128)S(1)} collective-permute-done((f32[2,64,2048]{2,1,0:T(8,128)}, f32[2,64,2048]{2,1,0:T(8,128)S(1)}, u32[]{:S(2)}, u32[]{:S(2)}) %collective-permute-start) | collective-permute-done | bytes 1048608 | tf_op jit(solution)/shard_map/ppermute | solution.py:471
  128.6 0.0 copy-start
  128.6 1.0 copy-done
  129.5 14.1 %join.1 = (f32[1,1,64,1024]{3,2,1,0:T(8,128)}, f32[1,1,64,1024]{3,2,1,0:T(8,128)}) custom-call(s32[1]{0:T(128)} %bitcast.refs_0_, f32[2,64,2048]{2,1,0:T(8,128)} %layer.1.refs_1_, f32[2,64,2048]{2,1,0:T(8,128)} %copy-done, bf16[128,2048]{1,0:T(8,128)(2,1)} %constant.9.clone.refs_4_.refs_3_), custom_call_target="tpu_custom_call" | custom-call | tf_op jit(solution)/shard_map/join/pallas_call | solution.py:474
Async XLA Ops:
  125.6 2.9 %collective-permute-start = (f32[2,64,2048]{2,1,0:T(8,128)}, f32[2,64,2048]{2,1,0:T(8,128)S(1)}, u32[]{:S(2)}, u32[]{:S(2)}) collective-permute-start(f32[2,64,2048]{2,1,0:T(8,128)} %layer.1.refs_1_), channel_id=1, source_target_pairs={{0,1},{1,0},{2,3},{3,2},{4,5},{5,4},{6,7},{7,6},{8,9},{9,8},{10,11... | collective-permute-start | bytes 3145736 | tf_op jit(solution)/shard_map/ppermute | solution.py:471
  128.6 1.0 copy-start
